TPU v7x, 32 devices: a whole 2x2x4 slice. The times are simulated.
32 devices in a mesh: seq: 16 (over z, x, core), head: 2 (over y).
Axes of the slice: x: 2, y: 2, z: 4, core: 2. Of those that a mesh axis runs over, the one named last changes fastest.
Arguments:
- query: bfloat16 [18432, 3072], P(('seq', 'head')), may hold values from -6 to 6
- keys: bfloat16 [18432, 3072], P(('seq', 'head')), may hold values from -6 to 6
- values: bfloat16 [18432, 3072], P(('seq', 'head')), may hold values from -6 to 6
- windows: int32 [48, 5], P('seq'), may hold values from -1 to 47, as said below
Outputs:
- attended: bfloat16 [18432, 3072], P(('seq', 'head'))
Inputs may be any that keep to these rules, and one draw needn't show every extreme that they name: `windows`: row t starts with t, then lists distinct tiles, then -1 in every remaining slot. Each listed tile other than t has a tile row within 1 of t's and lies either in t's tile-frame in t's tile column or the one beside it (tile column index within 1), or in t's tile column of the tile-frame before or after; so with s = t // 3 it lies in tile column s, s - 1, s + 1, s - 4 or s + 4.
All inputs are finite; a program needn't handle non-finite values.
Results may differ from a plain program's by a relative error of at most 0.0048.
Values may be sent and summed in bfloat16 or wider, within the bound.
A program may use at most 192 MiB of HBM per device.

v0:
```python
import jax
import jax.numpy as jnp
from jax import lax
from jax.sharding import PartitionSpec as P

HD = 128
TFR = 4


def from_behind(value, axis, by):
    peers = lax.axis_size(axis)
    pairs = [(i, i + by) for i in range(peers) if 0 <= i + by < peers]
    return lax.ppermute(value, axis, pairs)


def body(query, keys, values, windows):
    q_here, k_here, v_here = (
        lax.all_to_all(query, "head", split_axis=1, concat_axis=0, tiled=True),
        lax.all_to_all(keys, "head", split_axis=1, concat_axis=0, tiled=True),
        lax.all_to_all(values, "head", split_axis=1, concat_axis=0, tiled=True),
    )
    paired = jnp.concatenate([k_here, v_here], axis=1)
    columns = lax.axis_size("seq") // TFR
    neighbours = []
    for reach in (columns, 1, -1, -columns):
        neighbours.append(from_behind(paired, "seq", reach))
    slab = q_here.shape[0]
    local = q_here.shape[1]
    heads = local // HD
    per_slab = windows.shape[0]
    tile = slab // per_slab
    widened = jnp.concatenate(
        [neighbours[0], neighbours[1], paired, neighbours[2], neighbours[3]], axis=0
    )
    widened = widened.reshape(-1, tile, 2, heads, HD)
    own_column = lax.axis_index("seq")
    live = windows >= 0
    delta = windows // per_slab - own_column
    code = jnp.where(
        delta == -columns,
        0,
        jnp.where(delta == -1, 1, jnp.where(delta == 0, 2, jnp.where(delta == 1, 3, 4))),
    )
    slots = jnp.where(live, code * per_slab + windows % per_slab, 0)
    queries = q_here.reshape(per_slab, tile, heads, HD)
    scale = 1.0 / HD**0.5

    def one_tile(item):
        q_tile, row, row_live = item
        picked = jnp.take(widened, row, axis=0).reshape(-1, 2, heads, HD)
        scores = (
            jnp.einsum("qhd,khd->hqk", q_tile, picked[:, 0], preferred_element_type=jnp.float32)
            * scale
        )
        key_live = jnp.repeat(row_live, tile)
        scores = jnp.where(key_live[None, None, :], scores, -jnp.inf)
        top = jnp.max(scores, axis=-1, keepdims=True)
        expo = jnp.exp(scores - top)
        total = jnp.sum(expo, axis=-1)
        weights = expo.astype(jnp.bfloat16)
        mixed = jnp.einsum(
            "hqk,khd->qhd", weights, picked[:, 1], preferred_element_type=jnp.float32
        )
        return (mixed / jnp.transpose(total)[:, :, None]).astype(jnp.bfloat16)

    result = lax.map(one_tile, (queries, slots, live))
    result = result.reshape(slab, local)
    return lax.all_to_all(result, "head", split_axis=0, concat_axis=1, tiled=True)


def solution(mesh):
    return jax.shard_map(
        body,
        mesh=mesh,
        in_specs=(
            P(("seq", "head"), None),
            P(("seq", "head"), None),
            P(("seq", "head"), None),
            P("seq", None),
        ),
        out_specs=P(("seq", "head"), None),
        check_vma=False,
    )
```

profile of v0, /device:TPU:0, one launch (start us, length us, event | category | flops | bytes accessed | tf_op | source)
XLA Modules:
  0.0 889.9 jit_solution(2683900586914788517)
XLA Ops:
  12.3 37.5 %all-to-all-done = bf16[576,2,1536]{2,0,1:T(8,128)(2,1)S(1)} async-done(((bf16[576,2,1536]{2,0,1:T(8,128)(2,1)}), bf16[576,2,1536]{2,0,1:T(8,128)(2,1)S(1)}, u32[]{:S(2)}, u32[]{:S(2)}) %all-to-all-start) | async-done | bytes 3538976 | tf_op jit(solution)/shard_map/all_to_all | solution.py:19
  49.8 47.1 %all_to_all.73 = bf16[576,2,1536]{2,0,1:T(8,128)(2,1)} all-to-all(bf16[576,2,1536]{2,0,1:T(8,128)(2,1)} %bitcast.92), channel_id=1, replica_groups=mesh['seq'=16,'head'=2] {'head'}, dimensions={1} | all-to-all | bytes 7077888 | tf_op jit(solution)/shard_map/all_to_all | solution.py:20
  125.3 41.6 %all-to-all-done.2 = bf16[576,2,1536]{2,0,1:T(8,128)(2,1)} async-done(((bf16[576,2,1536]{2,0,1:T(8,128)(2,1)}), bf16[576,2,1536]{2,0,1:T(8,128)(2,1)}, u32[]{:S(2)}, u32[]{:S(2)}) %all-to-all-start.2) | async-done | bytes 3538976 | tf_op jit(solution)/shard_map/all_to_all | solution.py:18
  179.4 76.8 %collective-permute-done = bf16[1152,3072]{1,0:T(8,128)(2,1)} collective-permute-done((bf16[1152,3072]{1,0:T(8,128)(2,1)}, bf16[1152,3072]{1,0:T(8,128)(2,1)}, u32[]{:S(2)}, u32[]{:S(2)}) %collective-permute-start) | collective-permute-done | bytes 7077920 | tf_op jit(solution)/shard_map/ppermute | solution.py:13
  281.2 62.4 %collective-permute-done.3 = bf16[1152,3072]{1,0:T(8,128)(2,1)} collective-permute-done((bf16[1152,3072]{1,0:T(8,128)(2,1)}, bf16[1152,3072]{1,0:T(8,128)(2,1)}, u32[]{:S(2)}, u32[]{:S(2)}) %collective-permute-start.3) | collective-permute-done | bytes 7077920 | tf_op jit(solution)/shard_map/ppermute | solution.py:13
  350.2 60.9 %reshape.80 = bf16[15,384,2,12,128]{4,3,2,1,0:T(8,128)(2,1)} reshape(bf16[5760,3072]{1,0:T(8,128)(2,1)} %constant_dynamic-update-slice_fusion) | data formatting | bytes 70778880 | tf_op jit(solution)/shard_map/reshape | solution.py:35
  411.0 440.3 %while.10 = (s32[]{:T(128)}, bf16[3,384,12,128]{1,3,2,0:T(8,128)(2,1)S(1)}, s32[3,5]{1,0:T(4,128)S(1)}, bf16[15,384,2,12,128]{4,3,2,1,0:T(8,128)(2,1)}, pred[3,5...) while((s32[]{:T(128)}, bf16[3,384,12,128]{1,3,2,0:T(8,128)(2,1)S(1)}, ...), condition=%wide.region_3.4_spmd, body=%wide.region_0.3_spmd.sunk | while | flops 4640137216 | bytes 285603936 | solution.py:66
  411.1 21.6 %mini-gather-slice.5 = bf16[15,256,2,12,128]{4,3,2,1,0:T(8,128)(2,1)} slice(bf16[15,384,2,12,128]{4,3,2,1,0:T(8,128)(2,1)} %get-tuple-element.134), slice={[0:15], [0:256], [0:2], [0:12], [0:128]} | slice | bytes 47185920 | tf_op jit(solution)/shard_map/while/body/eval_jaxpr/jit(_take)/gather | solution.py:50
  432.7 15.3 %gather_fusion.1 = bf16[5,256,2,12,128]{4,3,2,1,0:T(8,128)(2,1)} fusion(bf16[15,256,2,12,128]{4,3,2,1,0:T(8,128)(2,1)} %mini-gather-slice.5, s32[1024]{0:T(1024)S(1)} %pad_clamp_fusion.2), kind=kCustom, calls=%fused_computation.clone.1 | custom fusion | bytes 15728660 | tf_op jit(solution)/shard_map/while/body/eval_jaxpr/jit(_take)/gather | solution.py:50
  447.9 14.2 %mini-gather-slice.4 = bf16[15,128,2,12,128]{4,3,2,1,0:T(8,128)(2,1)} slice(bf16[15,384,2,12,128]{4,3,2,1,0:T(8,128)(2,1)} %get-tuple-element.134), slice={[0:15], [256:384], [0:2], [0:12], [0:128]} | slice | bytes 23592960 | tf_op jit(solution)/shard_map/while/body/eval_jaxpr/jit(_take)/gather | solution.py:50
  471.3 11.3 %pad_maximum_fusion.3 = bf16[5,384,2,12,128]{4,3,2,1,0:T(8,128)(2,1)S(1)} fusion(bf16[5,128,2,12,128]{4,3,2,1,0:T(8,128)(2,1)} %gather_fusion, bf16[5,256,2,12,128]{4,3,2,1,0:T(8,128)(2,1)} %gather_fusion.1), kind=kLoop, calls=%fused_computation.9.clone.1 | loop fusion | flops 5898240 | bytes 23592960 | tf_op jit(solution)/shard_map/while
  482.6 13.6 %copy.58 = bf16[5,384,2,12,128]{4,1,0,3,2:T(8,128)(2,1)} copy(bf16[5,384,2,12,128]{4,3,2,1,0:T(8,128)(2,1)S(1)} %pad_maximum_fusion.3) | data formatting | bytes 23592960 | tf_op jit(solution)/shard_map/while
  507.0 17.0 %fusion.33 = (f32[12,384]{1,0:T(8,128)}, f32[12,384,1920]{2,1,0:T(8,128)}) fusion(pred[1920]{0:T(1024)(128)(4,1)S(1)} %broadcast_in_dim.104, bf16[1920,2,12,128]{3,0,2,1:T(8,128)(2,1)} %bitcast_select_fusion.2, bf16[3,384,12,128]{3,1,2,0:T(8,128)(2,1)} %get-tuple-element.136, s32[]{:T(128)} %get-tuple-element.124), kind=kOutput, calls=%fused_computation.4.clone.1 | convolution fusion | flops 2291461632 | bytes 42488192 | tf_op jit(solution)/shard_map/while/body/eval_jaxpr/qhd,khd->hqk/dot_general | solution.py:52
  524.0 16.1 %fusion.34 = f32[12,384]{1,0:T(8,128)} fusion(f32[12,384,1920]{2,1,0:T(8,128)} %get-tuple-element.115, f32[12,384]{1,0:T(8,128)} %get-tuple-element.116, pred[1920]{0:T(1024)(128)(4,1)S(1)} %broadcast_in_dim.104), kind=kLoop, calls=%fused_computation.5.clone.1 | loop fusion | flops 35384832 | bytes 35428224 | tf_op jit(solution)/shard_map/while/body/eval_jaxpr/reduce_sum | solution.py:59
  540.1 17.7 %fusion.35 = bf16[3,384,12,128]{1,3,2,0:T(8,128)(2,1)S(1)} fusion(bf16[3,384,12,128]{1,3,2,0:T(8,128)(2,1)S(1)} %get-tuple-element.125, s32[]{:T(128)} %get-tuple-element.124, f32[12,384,1920]{2,1,0:T(8,128)} %get-tuple-element.115, f32[12,384]{1,0:T(8,128)} %get-tuple-element.116, pred[1920]{0:T(1024)(128)(4,1)S(1)} %broadcast_in_dim.104, ...), kind=kOutput, calls=%fused_computation.17.clone.1 | convolution fusion | flops 2301493248 | bytes 42519040 | tf_op jit(solution)/shard_map/while/body/eval_jaxpr/hqk,khd->qhd/dot_general | solution.py:61
  557.9 21.6 %mini-gather-slice.5 = bf16[15,256,2,12,128]{4,3,2,1,0:T(8,128)(2,1)} slice(bf16[15,384,2,12,128]{4,3,2,1,0:T(8,128)(2,1)} %get-tuple-element.134), slice={[0:15], [0:256], [0:2], [0:12], [0:128]} | slice | bytes 47185920 | tf_op jit(solution)/shard_map/while/body/eval_jaxpr/jit(_take)/gather | solution.py:50
  579.5 15.3 %gather_fusion.1 = bf16[5,256,2,12,128]{4,3,2,1,0:T(8,128)(2,1)} fusion(bf16[15,256,2,12,128]{4,3,2,1,0:T(8,128)(2,1)} %mini-gather-slice.5, s32[1024]{0:T(1024)S(1)} %pad_clamp_fusion.2), kind=kCustom, calls=%fused_computation.clone.1 | custom fusion | bytes 15728660 | tf_op jit(solution)/shard_map/while/body/eval_jaxpr/jit(_take)/gather | solution.py:50
  594.7 14.2 %mini-gather-slice.4 = bf16[15,128,2,12,128]{4,3,2,1,0:T(8,128)(2,1)} slice(bf16[15,384,2,12,128]{4,3,2,1,0:T(8,128)(2,1)} %get-tuple-element.134), slice={[0:15], [256:384], [0:2], [0:12], [0:128]} | slice | bytes 23592960 | tf_op jit(solution)/shard_map/while/body/eval_jaxpr/jit(_take)/gather | solution.py:50
  618.1 11.3 %pad_maximum_fusion.3 = bf16[5,384,2,12,128]{4,3,2,1,0:T(8,128)(2,1)S(1)} fusion(bf16[5,128,2,12,128]{4,3,2,1,0:T(8,128)(2,1)} %gather_fusion, bf16[5,256,2,12,128]{4,3,2,1,0:T(8,128)(2,1)} %gather_fusion.1), kind=kLoop, calls=%fused_computation.9.clone.1 | loop fusion | flops 5898240 | bytes 23592960 | tf_op jit(solution)/shard_map/while
  629.4 13.6 %copy.58 = bf16[5,384,2,12,128]{4,1,0,3,2:T(8,128)(2,1)} copy(bf16[5,384,2,12,128]{4,3,2,1,0:T(8,128)(2,1)S(1)} %pad_maximum_fusion.3) | data formatting | bytes 23592960 | tf_op jit(solution)/shard_map/while
  653.8 17.0 %fusion.33 = (f32[12,384]{1,0:T(8,128)}, f32[12,384,1920]{2,1,0:T(8,128)}) fusion(pred[1920]{0:T(1024)(128)(4,1)S(1)} %broadcast_in_dim.104, bf16[1920,2,12,128]{3,0,2,1:T(8,128)(2,1)} %bitcast_select_fusion.2, bf16[3,384,12,128]{3,1,2,0:T(8,128)(2,1)} %get-tuple-element.136, s32[]{:T(128)} %get-tuple-element.124), kind=kOutput, calls=%fused_computation.4.clone.1 | convolution fusion | flops 2291461632 | bytes 42488192 | tf_op jit(solution)/shard_map/while/body/eval_jaxpr/qhd,khd->hqk/dot_general | solution.py:52
  670.8 16.1 %fusion.34 = f32[12,384]{1,0:T(8,128)} fusion(f32[12,384,1920]{2,1,0:T(8,128)} %get-tuple-element.115, f32[12,384]{1,0:T(8,128)} %get-tuple-element.116, pred[1920]{0:T(1024)(128)(4,1)S(1)} %broadcast_in_dim.104), kind=kLoop, calls=%fused_computation.5.clone.1 | loop fusion | flops 35384832 | bytes 35428224 | tf_op jit(solution)/shard_map/while/body/eval_jaxpr/reduce_sum | solution.py:59
  686.9 17.7 %fusion.35 = bf16[3,384,12,128]{1,3,2,0:T(8,128)(2,1)S(1)} fusion(bf16[3,384,12,128]{1,3,2,0:T(8,128)(2,1)S(1)} %get-tuple-element.125, s32[]{:T(128)} %get-tuple-element.124, f32[12,384,1920]{2,1,0:T(8,128)} %get-tuple-element.115, f32[12,384]{1,0:T(8,128)} %get-tuple-element.116, pred[1920]{0:T(1024)(128)(4,1)S(1)} %broadcast_in_dim.104, ...), kind=kOutput, calls=%fused_computation.17.clone.1 | convolution fusion | flops 2301493248 | bytes 42519040 | tf_op jit(solution)/shard_map/while/body/eval_jaxpr/hqk,khd->qhd/dot_general | solution.py:61
  704.7 21.6 %mini-gather-slice.5 = bf16[15,256,2,12,128]{4,3,2,1,0:T(8,128)(2,1)} slice(bf16[15,384,2,12,128]{4,3,2,1,0:T(8,128)(2,1)} %get-tuple-element.134), slice={[0:15], [0:256], [0:2], [0:12], [0:128]} | slice | bytes 47185920 | tf_op jit(solution)/shard_map/while/body/eval_jaxpr/jit(_take)/gather | solution.py:50
  726.3 15.3 %gather_fusion.1 = bf16[5,256,2,12,128]{4,3,2,1,0:T(8,128)(2,1)} fusion(bf16[15,256,2,12,128]{4,3,2,1,0:T(8,128)(2,1)} %mini-gather-slice.5, s32[1024]{0:T(1024)S(1)} %pad_clamp_fusion.2), kind=kCustom, calls=%fused_computation.clone.1 | custom fusion | bytes 15728660 | tf_op jit(solution)/shard_map/while/body/eval_jaxpr/jit(_take)/gather | solution.py:50
  741.5 14.2 %mini-gather-slice.4 = bf16[15,128,2,12,128]{4,3,2,1,0:T(8,128)(2,1)} slice(bf16[15,384,2,12,128]{4,3,2,1,0:T(8,128)(2,1)} %get-tuple-element.134), slice={[0:15], [256:384], [0:2], [0:12], [0:128]} | slice | bytes 23592960 | tf_op jit(solution)/shard_map/while/body/eval_jaxpr/jit(_take)/gather | solution.py:50
  764.8 11.3 %pad_maximum_fusion.3 = bf16[5,384,2,12,128]{4,3,2,1,0:T(8,128)(2,1)S(1)} fusion(bf16[5,128,2,12,128]{4,3,2,1,0:T(8,128)(2,1)} %gather_fusion, bf16[5,256,2,12,128]{4,3,2,1,0:T(8,128)(2,1)} %gather_fusion.1), kind=kLoop, calls=%fused_computation.9.clone.1 | loop fusion | flops 5898240 | bytes 23592960 | tf_op jit(solution)/shard_map/while
  776.1 13.6 %copy.58 = bf16[5,384,2,12,128]{4,1,0,3,2:T(8,128)(2,1)} copy(bf16[5,384,2,12,128]{4,3,2,1,0:T(8,128)(2,1)S(1)} %pad_maximum_fusion.3) | data formatting | bytes 23592960 | tf_op jit(solution)/shard_map/while
  800.5 17.0 %fusion.33 = (f32[12,384]{1,0:T(8,128)}, f32[12,384,1920]{2,1,0:T(8,128)}) fusion(pred[1920]{0:T(1024)(128)(4,1)S(1)} %broadcast_in_dim.104, bf16[1920,2,12,128]{3,0,2,1:T(8,128)(2,1)} %bitcast_select_fusion.2, bf16[3,384,12,128]{3,1,2,0:T(8,128)(2,1)} %get-tuple-element.136, s32[]{:T(128)} %get-tuple-element.124), kind=kOutput, calls=%fused_computation.4.clone.1 | convolution fusion | flops 2291461632 | bytes 42488192 | tf_op jit(solution)/shard_map/while/body/eval_jaxpr/qhd,khd->hqk/dot_general | solution.py:52
  817.5 16.1 %fusion.34 = f32[12,384]{1,0:T(8,128)} fusion(f32[12,384,1920]{2,1,0:T(8,128)} %get-tuple-element.115, f32[12,384]{1,0:T(8,128)} %get-tuple-element.116, pred[1920]{0:T(1024)(128)(4,1)S(1)} %broadcast_in_dim.104), kind=kLoop, calls=%fused_computation.5.clone.1 | loop fusion | flops 35384832 | bytes 35428224 | tf_op jit(solution)/shard_map/while/body/eval_jaxpr/reduce_sum | solution.py:59
  833.6 17.7 %fusion.35 = bf16[3,384,12,128]{1,3,2,0:T(8,128)(2,1)S(1)} fusion(bf16[3,384,12,128]{1,3,2,0:T(8,128)(2,1)S(1)} %get-tuple-element.125, s32[]{:T(128)} %get-tuple-element.124, f32[12,384,1920]{2,1,0:T(8,128)} %get-tuple-element.115, f32[12,384]{1,0:T(8,128)} %get-tuple-element.116, pred[1920]{0:T(1024)(128)(4,1)S(1)} %broadcast_in_dim.104, ...), kind=kOutput, calls=%fused_computation.17.clone.1 | convolution fusion | flops 2301493248 | bytes 42519040 | tf_op jit(solution)/shard_map/while/body/eval_jaxpr/hqk,khd->qhd/dot_general | solution.py:61
  862.3 25.4 %all_to_all.74 = bf16[2,576,1536]{2,1,0:T(8,128)(2,1)S(1)} all-to-all(bf16[2,576,1536]{2,1,0:T(8,128)(2,1)S(1)} %all_to_all.65), channel_id=1, replica_groups=mesh['seq'=16,'head'=2] {'head'}, dimensions={0} | all-to-all | bytes 7077888 | tf_op jit(solution)/shard_map/all_to_all | solution.py:68
  (59 shorter events, 157.8 us)
Async XLA Ops:
  4.0 45.8 %all-to-all-start = ((bf16[576,2,1536]{2,0,1:T(8,128)(2,1)}), bf16[576,2,1536]{2,0,1:T(8,128)(2,1)S(1)}, u32[]{:S(2)}, u32[]{:S(2)}) async-start(bf16[576,2,1536]{2,0,1:T(8,128)(2,1)} %bitcast.91), calls=%async_computation | async-start | bytes 7077888 | tf_op jit(solution)/shard_map/all_to_all | solution.py:19
  102.6 22.6 %copy-start.1 = (s32[3,5]{1,0:T(4,128)S(1)}, s32[3,5]{1,0:T(4,128)}, u32[]{:S(2)}) copy-start(s32[3,5]{1,0:T(4,128)} %param.9) | copy-start | bytes 184
  102.6 153.6 %collective-permute-start = (bf16[1152,3072]{1,0:T(8,128)(2,1)}, bf16[1152,3072]{1,0:T(8,128)(2,1)}, u32[]{:S(2)}, u32[]{:S(2)}) collective-permute-start(bf16[1152,3072]{1,0:T(8,128)(2,1)} %pad_maximum_fusion.1), channel_id=1, source_target_pairs={{0,8},{2,10},{4,12},{6,14},{8,16},{10,18},{12,20},{14,22},{16,24},... | collective-permute-start | bytes 21233672 | tf_op jit(solution)/shard_map/ppermute | solution.py:13
  109.0 153.7 %collective-permute-start.1 = (bf16[1152,3072]{1,0:T(8,128)(2,1)}, bf16[1152,3072]{1,0:T(8,128)(2,1)}, u32[]{:S(2)}, u32[]{:S(2)}) collective-permute-start(bf16[1152,3072]{1,0:T(8,128)(2,1)} %pad_maximum_fusion.1), channel_id=1, source_target_pairs={{0,2},{2,4},{4,6},{6,8},{8,10},{10,12},{12,14},{14,16},{16,18},{18... | collective-permute-start | bytes 21233672 | tf_op jit(solution)/shard_map/ppermute | solution.py:13
  113.2 161.6 %collective-permute-start.2 = (bf16[1152,3072]{1,0:T(8,128)(2,1)}, bf16[1152,3072]{1,0:T(8,128)(2,1)}, u32[]{:S(2)}, u32[]{:S(2)}) collective-permute-start(bf16[1152,3072]{1,0:T(8,128)(2,1)} %pad_maximum_fusion.1), channel_id=1, source_target_pairs={{2,0},{4,2},{6,4},{8,6},{10,8},{12,10},{14,12},{16,14},{18,16},{20... | collective-permute-start | bytes 21233672 | tf_op jit(solution)/shard_map/ppermute | solution.py:13
  114.5 229.1 %collective-permute-start.3 = (bf16[1152,3072]{1,0:T(8,128)(2,1)}, bf16[1152,3072]{1,0:T(8,128)(2,1)}, u32[]{:S(2)}, u32[]{:S(2)}) collective-permute-start(bf16[1152,3072]{1,0:T(8,128)(2,1)} %pad_maximum_fusion.1), channel_id=1, source_target_pairs={{8,0},{10,2},{12,4},{14,6},{16,8},{18,10},{20,12},{22,14},{24,16},... | collective-permute-start | bytes 21233672 | tf_op jit(solution)/shard_map/ppermute | solution.py:13
  119.9 46.9 %all-to-all-start.2 = ((bf16[576,2,1536]{2,0,1:T(8,128)(2,1)}), bf16[576,2,1536]{2,0,1:T(8,128)(2,1)}, u32[]{:S(2)}, u32[]{:S(2)}) async-start(bf16[576,2,1536]{2,0,1:T(8,128)(2,1)} %bitcast.90), calls=%async_computation.2 | async-start | bytes 7077888 | tf_op jit(solution)/shard_map/all_to_all | solution.py:18
  350.1 60.9 %copy-start = (bf16[3,384,12,128]{1,3,2,0:T(8,128)(2,1)S(1)}, bf16[3,384,12,128]{1,3,2,0:T(8,128)(2,1)}, u32[]{:S(2)}) copy-start(bf16[3,384,12,128]{1,3,2,0:T(8,128)(2,1)} %custom-call.5) | copy-start | bytes 10616836
where the time goes:
time: 901 us; the launch traced here: 890 us
  local copies, waits for them, and re-layouts  347 us (39%)
  waiting for transfers between devices  218 us (24%)
  other arithmetic  126 us (14%)
  matrix products  104 us (12%)
  blocking collectives  72.5 us (8%)
  starting transfers between devices  22.7 us (3%)
    gather x12, local copies, waits for them, and re-layouts, one_tile(): picked = jnp.take(widened, row, axis=0).reshape(-1, 2, heads, HD)  181 us
    ppermute x4, waiting for transfers between devices, from_behind(): return lax.ppermute(value, axis, pairs)  139 us
    reshape x1, local copies, waits for them, and re-layouts, body(): widened = widened.reshape(-1, tile, 2, heads, HD)  60.9 us
    dot_general x3, matrix products, one_tile(): jnp.einsum('hqk,khd->qhd', weights, picked[:, 1], preferred_element_type=...  53.1 us
    dot_general x3, matrix products, one_tile(): jnp.einsum('qhd,khd->hqk', q_tile, picked[:, 0], preferred_element_type=j...  51 us
    reduce_sum x3, other arithmetic, one_tile(): total = jnp.sum(expo, axis=-1)  48.4 us
    all_to_all x1, blocking collectives, body(): lax.all_to_all(values, 'head', split_axis=1, concat_axis=0, tiled=True)  47.1 us
    all_to_all x1, waiting for transfers between devices, body(): lax.all_to_all(query, 'head', split_axis=1, concat_axis=0, tiled=True)  41.6 us
  transfers between devices with their start and end apart: 6, of which 4 were waited for; matrix products, arithmetic and copies ran while one was open for 5% of the time, Pallas kernels for 0%

commit v1 on v0

v1 whole, which is shorter than its diff:
```python
import functools
import math

import jax
import jax.numpy as jnp
from jax import lax
from jax.experimental import pallas as pl
from jax.experimental.pallas import tpu as pltpu
from jax.sharding import PartitionSpec as P

HD = 128
TFR = 4
LOG2E = 1.4426950408889634
SLABS = 5
OWN = 2
AHEAD = 2


def group_sizes(heads):
    return [2] * (heads // 2) + [1] * (heads % 2)


def kernel(cfg, q_hbm, k_hbm, v_hbm, slots, offs, out, *scratch):
    seqs, peers, per_slab, tile, tokens, block, width, sizes = cfg
    n = len(sizes)
    starts = [sum(sizes[:g]) for g in range(n)]
    heads = sum(sizes)
    k_bufs, v_bufs = scratch[:n], scratch[n : 2 * n]
    (q_buf, o_buf, ex_send, ex_recv, kv_send, kv_recv, own_sem, o_send, o_recv, o_sem) = scratch[2 * n :]
    slab = per_slab * tile
    columns = seqs // TFR
    seq = lax.axis_index("seq")
    me = lax.axis_index("head")
    column = lax.rem(seq, columns)

    sends = [
        (seq + columns, 0, seq < seqs - columns),
        (seq + 1, 1, column < columns - 1),
        (seq - 1, 3, column > 0),
        (seq - columns, 4, seq >= columns),
    ]
    comes = [seq >= columns, column > 0, None, column < columns - 1, seq < seqs - columns]
    comes = [comes[code] for _, code, _ in sends]

    barrier = pltpu.get_barrier_semaphore()
    for p in range(1, peers):
        pl.semaphore_signal(
            barrier, inc=1, device_id={"head": lax.rem(me + p, peers)}, device_id_type=pl.DeviceIdType.MESH
        )
    count = peers - 1
    for target, _, there in sends:
        @pl.when(there)
        def _(target=target):
            pl.semaphore_signal(barrier, inc=1, device_id={"seq": target}, device_id_type=pl.DeviceIdType.MESH)

        count = count + there.astype(jnp.int32)
    pl.semaphore_wait(barrier, count)

    def rows_of(owner):
        return pl.ds(pl.multiple_of(owner * tokens, 16), tokens)

    def blocks_of(owner, code):
        return pl.ds((code * peers + owner) * (tokens // block), tokens // block)

    def slab_of(code):
        return pl.ds(code * (slab // block), slab // block)

    def lanes_in(owner, g):
        return pl.ds(pl.multiple_of((owner * heads + starts[g]) * HD, HD), sizes[g] * HD)

    def lanes_of(g):
        return pl.ds(starts[g] * HD, sizes[g] * HD)

    def place(g, which, owner):
        if which == 2:
            return q_buf.at[rows_of(owner), lanes_of(g)]
        return (k_bufs, v_bufs)[which][g].at[blocks_of(owner, OWN)]

    def source(which, owner, g):
        if which == 2:
            return q_hbm.at[:, lanes_in(owner, g)]
        return (k_hbm, v_hbm)[which].at[:, :, lanes_in(owner, g)]

    def exchange(g, which, p):
        to = lax.rem(me + p, peers)
        return pltpu.make_async_remote_copy(
            src_ref=source(which, to, g),
            dst_ref=place(g, which, me),
            send_sem=ex_send.at[g, which, p - 1],
            recv_sem=ex_recv.at[g, which, p - 1],
            device_id={"head": to},
            device_id_type=pl.DeviceIdType.MESH,
        )

    def own_copy(g, which):
        return pltpu.make_async_copy(source(which, me, g), place(g, which, me), own_sem.at[g, which])

    def onward(g, which, d, owner, from_hbm):
        target, code, _ = sends[d]
        buf = (k_bufs, v_bufs)[which][g]
        src = source(which, me, g) if from_hbm else place(g, which, owner)
        return pltpu.make_async_remote_copy(
            src_ref=src,
            dst_ref=buf.at[blocks_of(owner, code)],
            send_sem=kv_send.at[g, which, d],
            recv_sem=kv_recv.at[g, which, d],
            device_id={"seq": target},
            device_id_type=pl.DeviceIdType.MESH,
        )

    def whole(g, which, d):
        target, code, _ = sends[d]
        buf = (k_bufs, v_bufs)[which][g]
        return pltpu.make_async_remote_copy(
            src_ref=buf.at[slab_of(OWN)],
            dst_ref=buf.at[slab_of(code)],
            send_sem=kv_send.at[g, which, d],
            recv_sem=kv_recv.at[g, which, d],
            device_id={"seq": target},
            device_id_type=pl.DeviceIdType.MESH,
        )

    def issue(g):
        for which in range(2):
            for p in range(1, peers):
                exchange(g, which, p).start()
            for d in (0, 3, 1, 2):
                @pl.when(sends[d][2])
                def _(d=d, which=which):
                    onward(g, which, d, me, True).start()

            own_copy(g, which).start()
        for p in range(1, peers):
            exchange(g, 2, p).start()
        own_copy(g, 2).start()

    def forward(g):
        for which in range(2):
            for p in range(1, peers):
                exchange(g, which, p).wait_recv()
                owner = lax.rem(me - p + peers, peers)
                for d in (0, 3, 1, 2):
                    @pl.when(sends[d][2])
                    def _(d=d, which=which, owner=owner):
                        onward(g, which, d, owner, False).start()

    def o_copy(g, p):
        to = lax.rem(me + p, peers)
        return pltpu.make_async_remote_copy(
            src_ref=o_buf.at[rows_of(to), lanes_of(g)],
            dst_ref=out.at[:, lanes_in(me, g)],
            send_sem=o_send.at[g, p - 1],
            recv_sem=o_recv.at[g, p - 1],
            device_id={"head": to},
            device_id_type=pl.DeviceIdType.MESH,
        )

    def o_own(g):
        return pltpu.make_async_copy(
            o_buf.at[rows_of(me), lanes_of(g)], out.at[:, lanes_in(me, g)], o_sem.at[g]
        )

    def compute(g):
        for p in range(1, peers):
            exchange(g, 2, p).wait_recv()
        for which in range(3):
            own_copy(g, which).wait()
        for d in range(4):
            @pl.when(comes[d])
            def _(d=d):
                whole(g, 0, d).wait_recv()
                whole(g, 1, d).wait_recv()

        k_buf, v_buf = k_bufs[g], v_bufs[g]

        def step(i, carry):
            t = lax.div(i, sizes[g])
            h = lax.rem(i, sizes[g])
            lane = pl.ds(pl.multiple_of(h * HD, HD), HD)
            q_rows = pl.ds(pl.multiple_of(t * tile, tile), tile)
            q_lane = pl.ds(pl.multiple_of((starts[g] + h) * HD, HD), HD)
            q = q_buf[q_rows, q_lane]
            scores, picks = [], []
            top = None

            def tile_rows(buf, at):
                parts = [buf[at + b, :, lane] for b in range(tile // block)]
                return jnp.concatenate(parts, axis=0) if len(parts) > 1 else parts[0]

            for j in range(width):
                at = slots[t, j]
                s = lax.dot_general(
                    q, tile_rows(k_buf, at), (((1,), (1,)), ((), ())), preferred_element_type=jnp.float32
                )
                best = jnp.max(s, axis=1, keepdims=True) - offs[t, j]
                top = best if top is None else jnp.maximum(top, best)
                scores.append(s)
                picks.append(at)
            total = jnp.zeros((tile, 1), jnp.float32)
            mixed = jnp.zeros((tile, HD), jnp.float32)
            factor = LOG2E / HD**0.5
            for j in range(width):
                expo = jnp.exp2((scores[j] - (top + offs[t, j])) * factor)
                total = total + jnp.sum(expo, axis=1, keepdims=True)
                mixed = mixed + jnp.dot(
                    expo.astype(jnp.bfloat16), tile_rows(v_buf, picks[j]), preferred_element_type=jnp.float32
                )
            o_buf[q_rows, q_lane] = (mixed / total).astype(jnp.bfloat16)
            return carry

        lax.fori_loop(0, per_slab * sizes[g], step, 0)
        for p in range(1, peers):
            o_copy(g, p).start()
        o_own(g).start()

    for g in range(min(AHEAD, n)):
        issue(g)
    forward(0)
    for g in range(n):
        if g + AHEAD < n:
            issue(g + AHEAD)
        if g + 1 < n:
            forward(g + 1)
        compute(g)
    for g in range(n):
        for d in range(4):
            @pl.when(sends[d][2])
            def _(g=g, d=d):
                whole(g, 0, d).wait_send()
                whole(g, 1, d).wait_send()

        for p in range(1, peers):
            for which in range(3):
                exchange(g, which, p).wait_send()
            o_copy(g, p).wait()
        o_own(g).wait()


def body(query, keys, values, windows):
    seqs, peers = lax.axis_size("seq"), lax.axis_size("head")
    tokens, channels = query.shape
    per_slab, width = windows.shape
    slab = tokens * peers
    tile = slab // per_slab
    heads = channels // HD // peers
    sizes = group_sizes(heads)
    n = len(sizes)
    block = math.gcd(tokens, tile)
    cfg = (seqs, peers, per_slab, tile, tokens, block, width, sizes)
    kv = [pltpu.VMEM((SLABS * slab // block, block, size * HD), query.dtype) for size in sizes]
    columns = seqs // TFR
    seq = lax.axis_index("seq")
    live = windows >= 0
    at = jnp.where(live, windows, seq * per_slab)
    ahead = at // per_slab - seq
    code = jnp.where(ahead == 1, 3, jnp.where(ahead > 1, 4, OWN))
    code = jnp.where(ahead == -1, 1, jnp.where(ahead < -1, 0, code))
    slots = ((code * per_slab + at % per_slab) * (tile // block)).astype(jnp.int32)
    offs = jnp.where(live, 0.0, jnp.inf).astype(jnp.float32)
    others = peers - 1
    sem = pltpu.SemaphoreType.DMA
    pairs = per_slab * width * heads * tile * tile
    return pl.pallas_call(
        functools.partial(kernel, cfg),
        out_shape=jax.ShapeDtypeStruct(query.shape, query.dtype),
        in_specs=[pl.BlockSpec(memory_space=pl.ANY)] * 3 + [pl.BlockSpec(memory_space=pltpu.SMEM)] * 2,
        out_specs=pl.BlockSpec(memory_space=pl.ANY),
        scratch_shapes=kv
        + kv
        + [
            pltpu.VMEM((slab, heads * HD), query.dtype),
            pltpu.VMEM((slab, heads * HD), query.dtype),
            sem((n, 3, others)),
            sem((n, 3, others)),
            sem((n, 2, 4)),
            sem((n, 2, 4)),
            sem((n, 3)),
            sem((n, others)),
            sem((n, others)),
            sem((n,)),
        ],
        cost_estimate=pl.CostEstimate(
            flops=4 * pairs * HD, bytes_accessed=8 * tokens * channels, transcendentals=pairs
        ),
        compiler_params=pltpu.CompilerParams(
            collective_id=0, has_side_effects=True, vmem_limit_bytes=58 * 2**20
        ),
    )(
        query,
        keys.reshape(tokens // block, block, channels),
        values.reshape(tokens // block, block, channels),
        slots,
        offs,
    )


def solution(mesh):
    return jax.shard_map(
        body,
        mesh=mesh,
        in_specs=(
            P(("seq", "head"), None),
            P(("seq", "head"), None),
            P(("seq", "head"), None),
            P("seq", None),
        ),
        out_specs=P(("seq", "head"), None),
        check_vma=False,
    )
```

time: 901 us -> 183 us (0.20); the launches traced: 890 us -> 183 us
  local copies, waits for them, and re-layouts: 347 us -> 4.03 us
  waiting for transfers between devices: 218 us -> 0 us
  Pallas kernels: 0 us -> 176 us
  other arithmetic: 126 us -> 2.56 us
  matrix products: 104 us -> 0 us
  blocking collectives: 72.5 us -> 0 us
  starting transfers between devices: 22.7 us -> 0 us
    gather x12 -> x0, local copies, waits for them, and re-layouts: 181 us -> none  [one_tile(): picked = jnp.take(widened, row, axis=0).reshape(-1, 2, heads, HD)]
    pallas_call x0 -> x1, Pallas kernels: none -> 176 us  [body(): pl.pallas_call(functools.partial(kernel, cfg), out_shape=jax.ShapeDtypeSt...]
    ppermute x4 -> x0, waiting for transfers between devices: 139 us -> none  [from_behind(): return lax.ppermute(value, axis, pairs)]
    dot_general x6 -> x0, matrix products: 104 us -> none  [the longest x3 53.1 us: one_tile(): jnp.einsum('hqk,khd->qhd', weights, picked[:, 1], preferred_element_type=...]
    all_to_all x2 -> x0, waiting for transfers between devices: 79 us -> none  [the longest x1 41.6 us: body(): lax.all_to_all(query, 'head', split_axis=1, concat_axis=0, tiled=True)]
    all_to_all x2 -> x0, blocking collectives: 72.5 us -> none  [the longest x1 47.1 us: body(): lax.all_to_all(values, 'head', split_axis=1, concat_axis=0, tiled=True)]
    reshape x2 -> x0, local copies, waits for them, and re-layouts: 68.3 us -> none  [the longest x1 60.9 us: body(): widened = widened.reshape(-1, tile, 2, heads, HD)]
    while x5 -> x0, local copies, waits for them, and re-layouts: 51 us -> none
  transfers between devices with their start and end apart: 6 -> 0, of which waited for: 4 -> 0; matrix products, arithmetic and copies ran while one was open for 5% -> 0% of each run, Pallas kernels for 0% -> 0%
where the time goes in v1:
time: 183 us
  Pallas kernels  176 us (96%)
  local copies, waits for them, and re-layouts  4.03 us (2%)
  other arithmetic  2.56 us (1%)
    pallas_call x1, Pallas kernels, body(): pl.pallas_call(functools.partial(kernel, cfg), out_shape=jax.ShapeDtypeSt...  176 us
    unnamed x1, local copies, waits for them, and re-layouts  4.03 us

profile of v1, /device:TPU:0, one launch (start us, length us, event | category | flops | bytes accessed | tf_op | source)
XLA Modules:
  0.0 182.6 jit_solution(12942625076886202429)
XLA Ops:
  0.0 1.3 fusion.1.slots
  1.3 1.3 compare_select_fusion.offs
  2.6 176.0 %shard_map.46 = bf16[576,3072]{1,0:T(8,128)(2,1)} custom-call(bf16[576,3072]{1,0:T(8,128)(2,1)} %q_hbm.1, bf16[3,192,3072]{2,1,0:T(8,128)(2,1)} %bitcast.2, bf16[3,192,3072]{2,1,0:T(8,128)(2,1)} %bitcast.3, s32[3,5]{1,0:T(4,128)} %fusion.1.slots, f32[3,5]{1,0:T(4,128)} %compare_select_fusion.offs), custom_call_target="tpu_custom_call" | custom-call | flops 13589544960 | bytes 14155776 | tf_op jit(solution)/shard_map/pallas_call | solution.py:263
  178.6 4.0 %copy.6 = bf16[576,3072]{1,0:T(8,128)(2,1)} copy(bf16[576,3072]{1,0:T(8,128)(2,1)} %shard_map.46) | data formatting | bytes 7077888

commit v2 on v1

--- a/solution.py
+++ b/solution.py
@@ -13,14 +13,16 @@
 LOG2E = 1.4426950408889634
 SLABS = 5
 OWN = 2
-AHEAD = 2
+AHEAD = 4
+NEXT = 2
+DEAD = 3e38
 
 
 def group_sizes(heads):
-    return [2] * (heads // 2) + [1] * (heads % 2)
-
-
-def kernel(cfg, q_hbm, k_hbm, v_hbm, slots, offs, out, *scratch):
+    return [1] * heads
+
+
+def kernel(cfg, q_hbm, k_hbm, v_hbm, win, out, *scratch):
     seqs, peers, per_slab, tile, tokens, block, width, sizes = cfg
     n = len(sizes)
     starts = [sum(sizes[:g]) for g in range(n)]
@@ -121,18 +123,19 @@
         )
 
     def issue(g):
-        for which in range(2):
+        for which in range(3):
             for p in range(1, peers):
                 exchange(g, which, p).start()
+
+    def issue_own(g):
+        for which in range(2):
             for d in (0, 3, 1, 2):
                 @pl.when(sends[d][2])
                 def _(d=d, which=which):
                     onward(g, which, d, me, True).start()
 
+        for which in range(3):
             own_copy(g, which).start()
-        for p in range(1, peers):
-            exchange(g, 2, p).start()
-        own_copy(g, 2).start()
 
     def forward(g):
         for which in range(2):
@@ -175,12 +178,13 @@
 
         def step(i, carry):
             t = lax.div(i, sizes[g])
+            t = jnp.where(2 * me >= peers, t, per_slab - 1 - t)
             h = lax.rem(i, sizes[g])
             lane = pl.ds(pl.multiple_of(h * HD, HD), HD)
             q_rows = pl.ds(pl.multiple_of(t * tile, tile), tile)
             q_lane = pl.ds(pl.multiple_of((starts[g] + h) * HD, HD), HD)
             q = q_buf[q_rows, q_lane]
-            scores, picks = [], []
+            scores, picks, offs = [], [], []
             top = None
 
             def tile_rows(buf, at):
@@ -188,37 +192,57 @@
                 return jnp.concatenate(parts, axis=0) if len(parts) > 1 else parts[0]
 
             for j in range(width):
-                at = slots[t, j]
+                w = win[t, j]
+                live = w >= 0
+                key_tile = jnp.where(live, w, seq * per_slab)
+                ahead = lax.div(key_tile, per_slab) - seq
+                code = jnp.where(ahead == 1, 3, jnp.where(ahead > 1, 4, OWN))
+                code = jnp.where(ahead == -1, 1, jnp.where(ahead < -1, 0, code))
+                at = (code * per_slab + lax.rem(key_tile, per_slab)) * (tile // block)
+                off = jnp.where(live, 0.0, DEAD)
                 s = lax.dot_general(
                     q, tile_rows(k_buf, at), (((1,), (1,)), ((), ())), preferred_element_type=jnp.float32
                 )
-                best = jnp.max(s, axis=1, keepdims=True) - offs[t, j]
+                best = jnp.max(s, axis=1, keepdims=True) - off
                 top = best if top is None else jnp.maximum(top, best)
                 scores.append(s)
                 picks.append(at)
+                offs.append(off)
             total = jnp.zeros((tile, 1), jnp.float32)
             mixed = jnp.zeros((tile, HD), jnp.float32)
             factor = LOG2E / HD**0.5
             for j in range(width):
-                expo = jnp.exp2((scores[j] - (top + offs[t, j])) * factor)
+                expo = jnp.exp2((scores[j] - (top + offs[j])) * factor)
                 total = total + jnp.sum(expo, axis=1, keepdims=True)
                 mixed = mixed + jnp.dot(
                     expo.astype(jnp.bfloat16), tile_rows(v_buf, picks[j]), preferred_element_type=jnp.float32
                 )
             o_buf[q_rows, q_lane] = (mixed / total).astype(jnp.bfloat16)
+            if peers == 2:
+                @pl.when(i == early)
+                def _():
+                    o_copy(g, 1).start()
+
             return carry
 
+        early = ((per_slab + 1) // 2) * sizes[g] - 1
         lax.fori_loop(0, per_slab * sizes[g], step, 0)
-        for p in range(1, peers):
-            o_copy(g, p).start()
+        if peers != 2:
+            for p in range(1, peers):
+                o_copy(g, p).start()
         o_own(g).start()
 
-    for g in range(min(AHEAD, n)):
-        issue(g)
+    for g in range(max(AHEAD, NEXT)):
+        if g < min(AHEAD, n):
+            issue(g)
+        if g < min(NEXT, n):
+            issue_own(g)
     forward(0)
     for g in range(n):
         if g + AHEAD < n:
             issue(g + AHEAD)
+        if g + NEXT < n:
+            issue_own(g + NEXT)
         if g + 1 < n:
             forward(g + 1)
         compute(g)
@@ -248,22 +272,13 @@
     block = math.gcd(tokens, tile)
     cfg = (seqs, peers, per_slab, tile, tokens, block, width, sizes)
     kv = [pltpu.VMEM((SLABS * slab // block, block, size * HD), query.dtype) for size in sizes]
-    columns = seqs // TFR
-    seq = lax.axis_index("seq")
-    live = windows >= 0
-    at = jnp.where(live, windows, seq * per_slab)
-    ahead = at // per_slab - seq
-    code = jnp.where(ahead == 1, 3, jnp.where(ahead > 1, 4, OWN))
-    code = jnp.where(ahead == -1, 1, jnp.where(ahead < -1, 0, code))
-    slots = ((code * per_slab + at % per_slab) * (tile // block)).astype(jnp.int32)
-    offs = jnp.where(live, 0.0, jnp.inf).astype(jnp.float32)
     others = peers - 1
     sem = pltpu.SemaphoreType.DMA
     pairs = per_slab * width * heads * tile * tile
     return pl.pallas_call(
         functools.partial(kernel, cfg),
         out_shape=jax.ShapeDtypeStruct(query.shape, query.dtype),
-        in_specs=[pl.BlockSpec(memory_space=pl.ANY)] * 3 + [pl.BlockSpec(memory_space=pltpu.SMEM)] * 2,
+        in_specs=[pl.BlockSpec(memory_space=pl.ANY)] * 3 + [pl.BlockSpec(memory_space=pltpu.SMEM)],
         out_specs=pl.BlockSpec(memory_space=pl.ANY),
         scratch_shapes=kv
         + kv
@@ -289,8 +304,7 @@
         query,
         keys.reshape(tokens // block, block, channels),
         values.reshape(tokens // block, block, channels),
-        slots,
-        offs,
+        windows,
     )
 
 

time: 183 us -> 173 us (0.945)
  Pallas kernels: 176 us -> 169 us
  other arithmetic: 2.56 us -> 0 us
    pallas_call x1, Pallas kernels: 176 us -> 169 us  [body(): pl.pallas_call(functools.partial(kernel, cfg), out_shape=jax.ShapeDtypeSt...]
where the time goes in v2:
time: 173 us
  Pallas kernels  169 us (98%)
  local copies, waits for them, and re-layouts  4.03 us (2%)
    pallas_call x1, Pallas kernels, body(): pl.pallas_call(functools.partial(kernel, cfg), out_shape=jax.ShapeDtypeSt...  169 us
    unnamed x1, local copies, waits for them, and re-layouts  4.03 us

profile of v2, /device:TPU:0, one launch (start us, length us, event | category | flops | bytes accessed | tf_op | source)
XLA Modules:
  0.0 173.1 jit_solution(14826220683539153736)
XLA Ops:
  0.0 169.1 %shard_map.46 = bf16[576,3072]{1,0:T(8,128)(2,1)} custom-call(bf16[576,3072]{1,0:T(8,128)(2,1)} %q_hbm.1, bf16[3,192,3072]{2,1,0:T(8,128)(2,1)} %bitcast.2, bf16[3,192,3072]{2,1,0:T(8,128)(2,1)} %bitcast.3, s32[3,5]{1,0:T(4,128)} %win.1), custom_call_target="tpu_custom_call" | custom-call | flops 13589544960 | bytes 14155776 | tf_op jit(solution)/shard_map/pallas_call | solution.py:278
  169.1 4.0 %copy.6 = bf16[576,3072]{1,0:T(8,128)(2,1)} copy(bf16[576,3072]{1,0:T(8,128)(2,1)} %shard_map.46) | data formatting | bytes 7077888

commit v3 on v2

--- a/solution.py
+++ b/solution.py
@@ -123,9 +123,13 @@
         )
 
     def issue(g):
-        for which in range(3):
+        for which in range(2):
             for p in range(1, peers):
                 exchange(g, which, p).start()
+
+    def issue_query(g):
+        for p in range(1, peers):
+            exchange(g, 2, p).start()
 
     def issue_own(g):
         for which in range(2):
@@ -237,12 +241,14 @@
             issue(g)
         if g < min(NEXT, n):
             issue_own(g)
+            issue_query(g)
     forward(0)
     for g in range(n):
         if g + AHEAD < n:
             issue(g + AHEAD)
         if g + NEXT < n:
             issue_own(g + NEXT)
+            issue_query(g + NEXT)
         if g + 1 < n:
             forward(g + 1)
         compute(g)

time: 173 us -> 173 us (level)
  no operation moved by 1% of the time
where the time goes in v3:
time: 173 us
  Pallas kernels  169 us (98%)
  local copies, waits for them, and re-layouts  4.03 us (2%)
    pallas_call x1, Pallas kernels, body(): pl.pallas_call(functools.partial(kernel, cfg), out_shape=jax.ShapeDtypeSt...  169 us
    unnamed x1, local copies, waits for them, and re-layouts  4.03 us

profile of v3, /device:TPU:0, one launch (start us, length us, event | category | flops | bytes accessed | tf_op | source)
XLA Modules:
  0.0 173.1 jit_solution(2475026639440293118)
XLA Ops:
  0.0 169.1 %shard_map.46 = bf16[576,3072]{1,0:T(8,128)(2,1)} custom-call(bf16[576,3072]{1,0:T(8,128)(2,1)} %q_hbm.1, bf16[3,192,3072]{2,1,0:T(8,128)(2,1)} %bitcast.2, bf16[3,192,3072]{2,1,0:T(8,128)(2,1)} %bitcast.3, s32[3,5]{1,0:T(4,128)} %win.1), custom_call_target="tpu_custom_call" | custom-call | flops 13589544960 | bytes 14155776 | tf_op jit(solution)/shard_map/pallas_call | solution.py:284
  169.1 4.0 %copy.6 = bf16[576,3072]{1,0:T(8,128)(2,1)} copy(bf16[576,3072]{1,0:T(8,128)(2,1)} %shard_map.46) | data formatting | bytes 7077888
